TPU v7x, 128 devices: a whole 4x4x4 slice. The times are simulated.
128 devices in a mesh: row: 16 (over x, y), col: 8 (over z, core).
Axes of the slice: x: 4, y: 4, z: 4, core: 2. Of those that a mesh axis runs over, the one named last changes fastest.
Arguments:
- source_points: bfloat16 [65536, 1024], P('row'), may hold values from -8 to 8
- target_points: bfloat16 [32768, 1024], P('col', 'row'), may hold values from -8 to 8
- source_mass: float32 [65536], P('row'), may hold values from 0.25 to 4
- target_mass: float32 [32768], P('col'), may hold values from 0.25 to 4
- tile_index: int32 [256, 16], P('row', 'col'), may hold values from 0 to 15, as said below
- tile_count: int32 [256, 8], P('row', 'col'), may hold values from 1 to 2, as said below
Outputs:
- source_potential: float32 [65536], P('row')
- target_potential: float32 [32768], P('col')
Inputs may be any that keep to these rules, and one draw needn't show every extreme that they name: `tile_index`: within the 2 slots of one source tile and one index of col the target tiles are distinct; every target tile is named by a live slot of some source tile. `tile_count`: each index of row holds, for every index of col, a source tile with all 2 slots live.
All inputs are finite; a program needn't handle non-finite values.
Results may differ from a plain program's by a relative error of at most 0.0003.
Values may be sent and summed in bfloat16 or wider, within the bound.
A program may use at most 128 MiB of HBM per device.

v0:
```python
import math
import jax
import jax.numpy as jnp
from jax import lax
from jax.sharding import PartitionSpec as P

TILE = 256
ITERS = 3
masked_score = -1e30


def cost_terms(piece, source_points, tile_index):
    width = piece.shape[1]
    source_tiles = source_points.reshape(-1, TILE, width)
    target_tiles = piece.reshape(-1, TILE, width)
    chosen = target_tiles[tile_index]
    return jnp.einsum("rad,rkbd->rkab", source_tiles, chosen, preferred_element_type=jnp.float32)


def on_device(source_points, target_points, source_mass, target_mass, tile_index, tile_count):
    tiles_per_row = source_points.shape[0] // TILE
    col_tiles = target_points.shape[0] // TILE
    slot_count = tile_index.shape[1]
    scale = 1.0 / math.sqrt(source_points.shape[1])
    live = jnp.arange(slot_count)[None, :] < tile_count
    onehot = (tile_index[:, :, None] == jnp.arange(col_tiles)[None, None, :]) & live[:, :, None]
    log_source = jnp.log(source_mass).reshape(tiles_per_row, TILE)
    log_target = jnp.log(target_mass).reshape(col_tiles, TILE)
    target_pot = jnp.zeros((col_tiles, TILE), jnp.float32)
    source_pot = jnp.zeros((tiles_per_row, TILE), jnp.float32)
    for iteration in range(ITERS):
        cost = (
            cost_terms(
                lax.all_gather(target_points, "row", axis=1, tiled=True), source_points, tile_index
            )
            * scale
        )
        scores = cost + target_pot[tile_index][:, :, None, :]
        scores = jnp.where(live[:, :, None, None], scores, masked_score)
        row_top = jnp.max(scores, axis=(1, 3))
        highest = lax.pmax(row_top, "col")
        local_sum = jnp.sum(jnp.exp(scores - highest[:, None, :, None]), axis=(1, 3))
        total = lax.psum(local_sum, "col")
        source_pot = log_source - highest - jnp.log(total)
        columns = cost + source_pot[:, None, :, None]
        columns = jnp.where(live[:, :, None, None], columns, masked_score)
        slot_top = jnp.max(columns, axis=2)
        local_top = jnp.max(
            jnp.where(onehot[..., None], slot_top[:, :, None, :], masked_score), axis=(0, 1)
        )
        col_high = lax.pmax(local_top, "row")
        slot_ref = col_high[tile_index]
        sums = jnp.sum(jnp.exp(columns - slot_ref[:, :, None, :]), axis=2)
        col_sum = jnp.sum(jnp.where(onehot[..., None], sums[:, :, None, :], 0.0), axis=(0, 1))
        col_total = lax.psum(col_sum, "row")
        target_pot = log_target - col_high - jnp.log(col_total)
    return (source_pot.reshape(-1), target_pot.reshape(-1))


def solution(mesh):
    placed = (P("row", None), P("col", "row"), P("row"), P("col"), P("row", "col"), P("row", "col"))
    return jax.shard_map(
        on_device, mesh=mesh, in_specs=placed, out_specs=(P("row"), P("col")), check_vma=False
    )
```

profile of v0, /device:TPU:0, one launch (start us, length us, event | category | flops | bytes accessed | tf_op | source)
XLA Modules:
  0.0 747.5 jit_solution(9227641684370280702)
XLA Ops:
  12.5 70.8 %all-gather.2.cloned.1.call-done = bf16[4096,1024]{0,1:T(8,128)(2,1)} async-done(((bf16[4096,64]{0,1:T(8,128)(2,1)}), bf16[4096,1024]{0,1:T(8,128)(2,1)}) %all-gather.2.cloned.1.call-update) | async-done | bytes 8388624 | tf_op jit(solution)/shard_map/all_gather | solution.py:34
  83.2 12.0 %copy.14 = bf16[4096,1024]{1,0:T(8,128)(2,1)} copy(bf16[4096,1024]{0,1:T(8,128)(2,1)} %all-gather.2.cloned.1.call-done) | data formatting | bytes 16777216 | tf_op jit(solution)/shard_map/all_gather | solution.py:34
  95.2 10.6 %gather_fusion = bf16[32,256,1024]{2,1,0:T(8,128)(2,1)} fusion(bf16[16,256,1024]{2,1,0:T(8,128)(2,1)} %bitcast.57, s32[1024]{0:T(1024)S(1)} %pad_clamp_fusion), kind=kCustom, calls=%fused_computation | custom fusion | bytes 33554560 | tf_op jit(solution)/shard_map/gather | solution.py:16
  105.8 13.5 %bitcast_reduce_fusion.5 = (f32[16,256]{1,0:T(8,128)S(1)}, f32[16,2,256,256]{3,2,1,0:T(8,128)}) fusion(f32[16,2,256]{2,1,0:T(2,128)S(1)} %reshape.108, pred[16,2]{1,0:T(8,128)(4,1)S(1)} %iota_compare_fusion, bf16[16,2,256,1024]{3,2,1,0:T(8,128)(2,1)} %bitcast.58, bf16[16,256,1024,1]{2,1,3,0:T(8,128)(2,1)} %bitcast.63), kind=kOutput, calls=%fused_computation.28 | convolution fusion | flops 4303351808 | bytes 33603616 | tf_op jit(solution)/shard_map/rad,rkbd->rkab/dot_general | solution.py:17
  119.3 25.8 %pmax.42 = f32[16,256]{1,0:T(8,128)S(1)} all-reduce(f32[16,256]{1,0:T(8,128)S(1)} %get-tuple-element.2), channel_id=1, replica_groups=mesh['row'=16,'col'=8] {'col'}, use_global_device_ids=true, to_apply=%region_1.2 | all-reduce | flops 4096 | bytes 32768 | tf_op jit(solution)/shard_map/pmax | solution.py:41
  145.1 4.6 fusion.11
  149.8 23.6 %psum.42 = f32[16,256]{1,0:T(8,128)S(1)} all-reduce(f32[16,256]{1,0:T(8,128)S(1)} %fusion.11), channel_id=1, replica_groups=mesh['row'=16,'col'=8] {'col'}, use_global_device_ids=true, to_apply=%region_3.4 | all-reduce | flops 4096 | bytes 32768 | tf_op jit(solution)/shard_map/psum | solution.py:43
  173.3 4.7 bitcast_reduce_fusion.4
  178.1 72.4 %pmax.43 = f32[16,256]{1,0:T(8,128)S(1)} all-reduce(f32[16,256]{1,0:T(8,128)S(1)} %select_reduce_fusion.5), channel_id=1, replica_groups=mesh['row'=16,'col'=8] {'row'}, use_global_device_ids=true, to_apply=%region_6.7 | all-reduce | flops 4096 | bytes 32768 | tf_op jit(solution)/shard_map/pmax | solution.py:51
  251.1 5.1 fusion.9
  256.4 69.5 %psum.43 = f32[16,256]{1,0:T(8,128)S(1)} all-reduce(f32[16,256]{1,0:T(8,128)S(1)} %select_reduce_fusion.4), channel_id=1, replica_groups=mesh['row'=16,'col'=8] {'row'}, use_global_device_ids=true, to_apply=%region_9.10 | all-reduce | flops 4096 | bytes 32768 | tf_op jit(solution)/shard_map/psum | solution.py:55
  331.0 23.7 %pmax.44 = f32[16,256]{1,0:T(8,128)S(1)} all-reduce(f32[16,256]{1,0:T(8,128)S(1)} %bitcast_reduce_fusion.3), channel_id=1, replica_groups=mesh['row'=16,'col'=8] {'col'}, use_global_device_ids=true, to_apply=%region_11.12 | all-reduce | flops 4096 | bytes 32768 | tf_op jit(solution)/shard_map/pmax | solution.py:41
  354.8 4.6 fusion.7
  359.4 23.6 %psum.44 = f32[16,256]{1,0:T(8,128)S(1)} all-reduce(f32[16,256]{1,0:T(8,128)S(1)} %fusion.7), channel_id=1, replica_groups=mesh['row'=16,'col'=8] {'col'}, use_global_device_ids=true, to_apply=%region_13.14 | all-reduce | flops 4096 | bytes 32768 | tf_op jit(solution)/shard_map/psum | solution.py:43
  383.0 4.7 bitcast_reduce_fusion.2
  387.8 69.5 %pmax.45 = f32[16,256]{1,0:T(8,128)S(1)} all-reduce(f32[16,256]{1,0:T(8,128)S(1)} %select_reduce_fusion.3), channel_id=1, replica_groups=mesh['row'=16,'col'=8] {'row'}, use_global_device_ids=true, to_apply=%region_16.17 | all-reduce | flops 4096 | bytes 32768 | tf_op jit(solution)/shard_map/pmax | solution.py:51
  458.0 5.1 fusion.5
  463.2 69.5 %psum.45 = f32[16,256]{1,0:T(8,128)S(1)} all-reduce(f32[16,256]{1,0:T(8,128)S(1)} %select_reduce_fusion.2), channel_id=1, replica_groups=mesh['row'=16,'col'=8] {'row'}, use_global_device_ids=true, to_apply=%region_19.20 | all-reduce | flops 4096 | bytes 32768 | tf_op jit(solution)/shard_map/psum | solution.py:55
  537.8 23.6 %pmax.46 = f32[16,256]{1,0:T(8,128)S(1)} all-reduce(f32[16,256]{1,0:T(8,128)S(1)} %bitcast_reduce_fusion.1), channel_id=1, replica_groups=mesh['row'=16,'col'=8] {'col'}, use_global_device_ids=true, to_apply=%region_21.22 | all-reduce | flops 4096 | bytes 32768 | tf_op jit(solution)/shard_map/pmax | solution.py:41
  566.0 23.6 %psum.46 = f32[16,256]{1,0:T(8,128)S(1)} all-reduce(f32[16,256]{1,0:T(8,128)S(1)} %fusion.3), channel_id=1, replica_groups=mesh['row'=16,'col'=8] {'col'}, use_global_device_ids=true, to_apply=%region_23.24 | all-reduce | flops 4096 | bytes 32768 | tf_op jit(solution)/shard_map/psum | solution.py:43
  589.6 4.7 bitcast_reduce_fusion
  594.4 69.5 %pmax.47 = f32[16,256]{1,0:T(8,128)S(1)} all-reduce(f32[16,256]{1,0:T(8,128)S(1)} %select_reduce_fusion.1), channel_id=1, replica_groups=mesh['row'=16,'col'=8] {'row'}, use_global_device_ids=true, to_apply=%region_26.27 | all-reduce | flops 4096 | bytes 32768 | tf_op jit(solution)/shard_map/pmax | solution.py:51
  664.6 5.1 fusion.1
  669.8 69.5 %psum.47 = f32[16,256]{1,0:T(8,128)S(1)} all-reduce(f32[16,256]{1,0:T(8,128)S(1)} %select_reduce_fusion), channel_id=1, replica_groups=mesh['row'=16,'col'=8] {'row'}, use_global_device_ids=true, to_apply=%region_29.30 | all-reduce | flops 4096 | bytes 32768 | tf_op jit(solution)/shard_map/psum | solution.py:55
  (43 shorter events, 24.0 us)
Async XLA Ops:
  7.2 76.1 %all-gather.2.cloned.1.call-start = ((), (), s32[]{:S(2)}) async-start(), calls=%async_computation | async-start | bytes 8912896 | tf_op jit(solution)/shard_map/all_gather | solution.py:34
Sparse Core Ops, SparseCore 0:
  10.1 73.0 all-gather.1
where the time goes:
time: 748 us; the launch traced here: 747 us
  blocking collectives  564 us (75%)
  waiting for transfers between devices  71.4 us (10%)
  other arithmetic  54.5 us (7%)
  local copies, waits for them, and re-layouts  30 us (4%)
  between operations  14.3 us (2%)
  matrix products  13.5 us (2%)
    pmax x3, blocking collectives, on_device(): col_high = lax.pmax(local_top, 'row')  211 us
    psum x3, blocking collectives, on_device(): col_total = lax.psum(col_sum, 'row')  209 us
    pmax x3, blocking collectives, on_device(): highest = lax.pmax(row_top, 'col')  73.1 us
    all_gather x1, waiting for transfers between devices, on_device(): lax.all_gather(target_points, 'row', axis=1, tiled=True)  70.8 us
    psum x3, blocking collectives, on_device(): total = lax.psum(local_sum, 'col')  70.7 us
    reduce_sum x3, other arithmetic, on_device(): sums = jnp.sum(jnp.exp(columns - slot_ref[:, :, None, :]), axis=2)  15.4 us
  transfers between devices with their start and end apart: 1, of which 1 were waited for; matrix products, arithmetic and copies ran while one was open for 1% of the time, Pallas kernels for 0%

commit v1 on v0

--- a/solution.py
+++ b/solution.py
@@ -40,7 +40,7 @@
         row_top = jnp.max(scores, axis=(1, 3))
         highest = lax.pmax(row_top, "col")
         local_sum = jnp.sum(jnp.exp(scores - highest[:, None, :, None]), axis=(1, 3))
-        total = lax.psum(local_sum, "col")
+        total = jnp.sum(jax.lax.all_gather(local_sum, "col"), axis=0)
         source_pot = log_source - highest - jnp.log(total)
         columns = cost + source_pot[:, None, :, None]
         columns = jnp.where(live[:, :, None, None], columns, masked_score)

time: 748 us -> 716 us (0.957)
  blocking collectives: 564 us -> 531 us
    psum x3 -> x0, blocking collectives: 70.7 us -> none  [on_device(): total = lax.psum(local_sum, 'col')]
    all_gather x0 -> x3, blocking collectives: none -> 38.3 us  [on_device(): total = jnp.sum(jax.lax.all_gather(local_sum, 'col'), axis=0)]
where the time goes in v1:
time: 716 us; the launch traced here: 715 us
  blocking collectives  531 us (74%)
  waiting for transfers between devices  71.4 us (10%)
  other arithmetic  54.6 us (8%)
  local copies, waits for them, and re-layouts  30 us (4%)
  between operations  14.3 us (2%)
  matrix products  13.5 us (2%)
    pmax x3, blocking collectives, on_device(): col_high = lax.pmax(local_top, 'row')  211 us
    psum x3, blocking collectives, on_device(): col_total = lax.psum(col_sum, 'row')  209 us
    pmax x3, blocking collectives, on_device(): highest = lax.pmax(row_top, 'col')  73.1 us
    all_gather x1, waiting for transfers between devices, on_device(): lax.all_gather(target_points, 'row', axis=1, tiled=True)  70.8 us
    all_gather x3, blocking collectives, on_device(): total = jnp.sum(jax.lax.all_gather(local_sum, 'col'), axis=0)  38.3 us
    reduce_sum x3, other arithmetic, on_device(): sums = jnp.sum(jnp.exp(columns - slot_ref[:, :, None, :]), axis=2)  15.4 us
  transfers between devices with their start and end apart: 1, of which 1 were waited for; matrix products, arithmetic and copies ran while one was open for 1% of the time, Pallas kernels for 0%

profile of v1, /device:TPU:0, one launch (start us, length us, event | category | flops | bytes accessed | tf_op | source)
XLA Modules:
  0.0 715.2 jit_solution(16532274899149751317)
XLA Ops:
  12.5 70.8 %all-gather.5.cloned.1.call-done = bf16[4096,1024]{0,1:T(8,128)(2,1)} async-done(((bf16[4096,64]{0,1:T(8,128)(2,1)}), bf16[4096,1024]{0,1:T(8,128)(2,1)}) %all-gather.5.cloned.1.call-update) | async-done | bytes 8388624 | tf_op jit(solution)/shard_map/all_gather | solution.py:34
  83.2 12.0 %copy.14 = bf16[4096,1024]{1,0:T(8,128)(2,1)} copy(bf16[4096,1024]{0,1:T(8,128)(2,1)} %all-gather.5.cloned.1.call-done) | data formatting | bytes 16777216 | tf_op jit(solution)/shard_map/all_gather | solution.py:34
  95.2 10.6 %gather_fusion = bf16[32,256,1024]{2,1,0:T(8,128)(2,1)} fusion(bf16[16,256,1024]{2,1,0:T(8,128)(2,1)} %bitcast.60, s32[1024]{0:T(1024)S(1)} %pad_clamp_fusion), kind=kCustom, calls=%fused_computation | custom fusion | bytes 33554560 | tf_op jit(solution)/shard_map/gather | solution.py:16
  105.8 13.5 %bitcast_reduce_fusion.5 = (f32[16,256]{1,0:T(8,128)S(1)}, f32[16,2,256,256]{3,2,1,0:T(8,128)}) fusion(f32[16,2,256]{2,1,0:T(2,128)S(1)} %reshape.108, pred[16,2]{1,0:T(8,128)(4,1)S(1)} %iota_compare_fusion, bf16[16,2,256,1024]{3,2,1,0:T(8,128)(2,1)} %bitcast.61, bf16[16,256,1024,1]{2,1,3,0:T(8,128)(2,1)} %bitcast.69), kind=kOutput, calls=%fused_computation.28 | convolution fusion | flops 4303351808 | bytes 33603616 | tf_op jit(solution)/shard_map/rad,rkbd->rkab/dot_general | solution.py:17
  119.3 25.8 %pmax.42 = f32[16,256]{1,0:T(8,128)S(1)} all-reduce(f32[16,256]{1,0:T(8,128)S(1)} %get-tuple-element.2), channel_id=1, replica_groups=mesh['row'=16,'col'=8] {'col'}, use_global_device_ids=true, to_apply=%region_1.2 | all-reduce | flops 4096 | bytes 32768 | tf_op jit(solution)/shard_map/pmax | solution.py:41
  145.1 4.7 fusion.11
  149.8 12.8 %all-gather = f32[128,256]{1,0:T(8,128)S(1)} all-gather(f32[16,256]{1,0:T(8,128)S(1)} %fusion.11), channel_id=2, replica_groups=mesh['row'=16,'col'=8] {'col'}, dimensions={0}, use_global_device_ids=true | all-gather | bytes 147456 | tf_op jit(solution)/shard_map/all_gather | solution.py:43
  162.6 4.7 bitcast_reduce_fusion.4
  167.4 72.4 %pmax.43 = f32[16,256]{1,0:T(8,128)S(1)} all-reduce(f32[16,256]{1,0:T(8,128)S(1)} %select_reduce_fusion.5), channel_id=1, replica_groups=mesh['row'=16,'col'=8] {'row'}, use_global_device_ids=true, to_apply=%region_6.7 | all-reduce | flops 4096 | bytes 32768 | tf_op jit(solution)/shard_map/pmax | solution.py:51
  240.4 5.1 fusion.9
  245.7 69.5 %psum.21 = f32[16,256]{1,0:T(8,128)S(1)} all-reduce(f32[16,256]{1,0:T(8,128)S(1)} %select_reduce_fusion.4), channel_id=1, replica_groups=mesh['row'=16,'col'=8] {'row'}, use_global_device_ids=true, to_apply=%region_9.10 | all-reduce | flops 4096 | bytes 32768 | tf_op jit(solution)/shard_map/psum | solution.py:55
  320.3 23.7 %pmax.44 = f32[16,256]{1,0:T(8,128)S(1)} all-reduce(f32[16,256]{1,0:T(8,128)S(1)} %bitcast_reduce_fusion.3), channel_id=1, replica_groups=mesh['row'=16,'col'=8] {'col'}, use_global_device_ids=true, to_apply=%region_11.12 | all-reduce | flops 4096 | bytes 32768 | tf_op jit(solution)/shard_map/pmax | solution.py:41
  344.0 4.6 fusion.7
  348.7 12.8 %all-gather.1 = f32[128,256]{1,0:T(8,128)S(1)} all-gather(f32[16,256]{1,0:T(8,128)S(1)} %fusion.7), channel_id=3, replica_groups=mesh['row'=16,'col'=8] {'col'}, dimensions={0}, use_global_device_ids=true | all-gather | bytes 147456 | tf_op jit(solution)/shard_map/all_gather | solution.py:43
  361.4 4.7 bitcast_reduce_fusion.2
  366.3 69.5 %pmax.45 = f32[16,256]{1,0:T(8,128)S(1)} all-reduce(f32[16,256]{1,0:T(8,128)S(1)} %select_reduce_fusion.3), channel_id=1, replica_groups=mesh['row'=16,'col'=8] {'row'}, use_global_device_ids=true, to_apply=%region_16.17 | all-reduce | flops 4096 | bytes 32768 | tf_op jit(solution)/shard_map/pmax | solution.py:51
  436.4 5.1 fusion.5
  441.7 69.5 %psum.22 = f32[16,256]{1,0:T(8,128)S(1)} all-reduce(f32[16,256]{1,0:T(8,128)S(1)} %select_reduce_fusion.2), channel_id=1, replica_groups=mesh['row'=16,'col'=8] {'row'}, use_global_device_ids=true, to_apply=%region_19.20 | all-reduce | flops 4096 | bytes 32768 | tf_op jit(solution)/shard_map/psum | solution.py:55
  516.3 23.6 %pmax.46 = f32[16,256]{1,0:T(8,128)S(1)} all-reduce(f32[16,256]{1,0:T(8,128)S(1)} %bitcast_reduce_fusion.1), channel_id=1, replica_groups=mesh['row'=16,'col'=8] {'col'}, use_global_device_ids=true, to_apply=%region_21.22 | all-reduce | flops 4096 | bytes 32768 | tf_op jit(solution)/shard_map/pmax | solution.py:41
  544.5 12.8 %all-gather.2 = f32[128,256]{1,0:T(8,128)S(1)} all-gather(f32[16,256]{1,0:T(8,128)S(1)} %fusion.3), channel_id=4, replica_groups=mesh['row'=16,'col'=8] {'col'}, dimensions={0}, use_global_device_ids=true | all-gather | bytes 147456 | tf_op jit(solution)/shard_map/all_gather | solution.py:43
  557.3 4.7 bitcast_reduce_fusion
  562.1 69.5 %pmax.47 = f32[16,256]{1,0:T(8,128)S(1)} all-reduce(f32[16,256]{1,0:T(8,128)S(1)} %select_reduce_fusion.1), channel_id=1, replica_groups=mesh['row'=16,'col'=8] {'row'}, use_global_device_ids=true, to_apply=%region_26.27 | all-reduce | flops 4096 | bytes 32768 | tf_op jit(solution)/shard_map/pmax | solution.py:51
  632.3 5.1 fusion.1
  637.5 69.5 %psum.23 = f32[16,256]{1,0:T(8,128)S(1)} all-reduce(f32[16,256]{1,0:T(8,128)S(1)} %select_reduce_fusion), channel_id=1, replica_groups=mesh['row'=16,'col'=8] {'row'}, use_global_device_ids=true, to_apply=%region_29.30 | all-reduce | flops 4096 | bytes 32768 | tf_op jit(solution)/shard_map/psum | solution.py:55
  (46 shorter events, 24.0 us)
Async XLA Ops:
  7.2 76.1 %all-gather.5.cloned.1.call-start = ((), (), s32[]{:S(2)}) async-start(), calls=%async_computation | async-start | bytes 8912896 | tf_op jit(solution)/shard_map/all_gather | solution.py:34
Sparse Core Ops, SparseCore 0:
  10.1 73.0 all-gather.4
